TPU v7x, 32 devices: a whole 2x2x4 slice. The times are simulated.
32 devices in a mesh: grp: 2 (over y), slab: 2 (over x), lat: 8 (over z, core).
Axes of the slice: x: 2, y: 2, z: 4, core: 2. Of those that a mesh axis runs over, the one named last changes fastest.
Arguments:
- cond_lists: int32 [64, 16], P(('slab', 'lat')), may hold values from 0 to 31, all different within a row
- regress: float32 [64, 128, 2048], P(('slab', 'lat')), may hold values from -0.09375 to 0.09375
- chol: float32 [64, 128, 128], P(('slab', 'lat')), as said below
- noise: float32 [128, 256, 128], P(('grp', 'slab', 'lat')), parts along dimension 0, may hold values from -6 to 6
- start_field: float32 [64, 256, 128], P(('grp', 'lat')), parts along dimension 0, may hold values from -6 to 6
Outputs:
- field: float32 [128, 256, 128], P(('grp', 'slab', 'lat')), parts along dimension 0
There are 2 independent parts, one for each index of `grp`. A program takes and returns all parts, laid end to end along the dimension named above; an argument that names none is the same for every part. Nothing has to cross between parts.
Inputs may be any that keep to these rules, and one draw needn't show every extreme that they name: `cond_lists`: each row names 16 distinct positions of the previous slab. `chol`: each factor is lower triangular with diagonal entries from 0.3 to 0.7.
All inputs are finite; a program needn't handle non-finite values.
Results may differ from a plain program's by a relative error of at most 0.0001.
Values sent between devices are 32-bit elements; how exact they have to be, the bound alone decides.
A program may use at most 64 MiB of HBM per device.

v0:
```python
import jax
import jax.numpy as jnp
from jax import lax
from jax.sharding import PartitionSpec as P

PANEL = 64


def passed_along(array, axis, by):
    length = lax.axis_size(axis)
    pairs = [(i, i + by) for i in range(length) if 0 <= i + by < length]
    return lax.ppermute(array, axis, pairs)


def shards(cond_lists, regress, chol, noise, start_field):
    blocks, nreal_here, block_size = noise.shape
    list_length = cond_lists.shape[1]
    front_width = PANEL
    fronts = nreal_here // front_width
    n_slab = lax.axis_size("slab")
    slab_pos = lax.axis_index("slab")
    sections = n_slab + fronts - 1
    factors = regress.reshape(blocks, block_size, list_length, block_size)

    def compute(front_start, previous):
        picked = previous[cond_lists]
        shocks = lax.dynamic_slice_in_dim(noise, front_start, front_width, 1)
        mean_part = jnp.einsum("jakb,jkwb->jwa", factors, picked, precision=lax.Precision.HIGHEST)
        shock_part = jnp.einsum("jab,jwb->jwa", chol, shocks, precision=lax.Precision.HIGHEST)
        return mean_part + shock_part

    def skip(front_start, previous):
        return jnp.zeros((blocks, front_width, block_size), jnp.float32)

    start_box = jnp.zeros((blocks, front_width, block_size), jnp.float32)

    def section(section_step, carry):
        incoming, field_out = carry
        front_index = section_step - slab_pos
        active = (front_index >= 0) & (front_index < fronts)
        front_start = jnp.clip(front_index, 0, fronts - 1) * front_width
        boundary = lax.dynamic_slice_in_dim(start_field, front_start, front_width, 1)
        source = jnp.where(slab_pos == 0, boundary, incoming)
        previous = lax.all_gather(source, "lat", axis=0, tiled=True)
        fresh_blocks = lax.cond(active, compute, skip, front_start, previous)
        old_blocks = lax.dynamic_slice_in_dim(field_out, front_start, front_width, 1)
        kept = jnp.where(active, fresh_blocks, old_blocks)
        field_out = lax.dynamic_update_slice_in_dim(field_out, kept, front_start, 1)
        incoming = passed_along(fresh_blocks, "slab", 1)
        return (incoming, field_out)

    start_out = jnp.zeros((blocks, nreal_here, block_size), jnp.float32)
    incoming, field_out = lax.fori_loop(0, sections, section, (start_box, start_out))
    return field_out


def solution(mesh):
    in_specs = (
        P(("slab", "lat"), None),
        P(("slab", "lat"), None, None),
        P(("slab", "lat"), None, None),
        P(("grp", "slab", "lat"), None, None),
        P(("grp", "lat"), None, None),
    )
    out_specs = P(("grp", "slab", "lat"), None, None)
    return jax.shard_map(shards, mesh=mesh, in_specs=in_specs, out_specs=out_specs, check_vma=False)
```

profile of v0, /device:TPU:3, one launch (start us, length us, event | category | flops | bytes accessed | tf_op | source)
XLA Modules:
  0.0 230.7 jit_solution(2512306260924469446)
XLA Ops:
  6.5 5.4 %copy.8 = f32[4,128,2048]{1,2,0:T(8,128)} copy(f32[4,128,2048]{2,1,0:T(8,128)} %param.10) | data formatting | bytes 8388608 | tf_op args[1]
  11.9 0.0 copy-start
  11.9 0.0 copy-start.2
  11.9 5.4 %copy.9 = f32[4,128,16,128]{3,1,2,0:T(8,128)} copy(f32[4,128,16,128]{1,3,2,0:T(8,128)} %bitcast.9) | data formatting | bytes 8388608 | tf_op jit(solution)/shard_map/while | solution.py:53
  17.3 0.0 copy-done
  17.3 0.0 copy-done.2
  17.4 206.1 %while.16 = (s32[]{:T(128)}, f32[4,64,128]{2,1,0:T(8,128)S(1)}, f32[4,256,128]{2,1,0:T(8,128)S(1)}, s32[]{:T(128)}, pred[]{:T(512)}, /*index=5*/f32[4,256,128]{2...) while((s32[]{:T(128)}, f32[4,64,128]{2,1,0:T(8,128)S(1)}, ...), condition=%wide.region_3.4_spmd, body=%wide.region_0.3_spmd.sunk | while | flops 855737536 | bytes 16127929 | solution.py:53
  17.4 0.0 all-gather.2.cloned.1.call-start
  17.4 1.6 dynamic-slice_select_fusion.2
  19.0 0.0 all-gather.2.cloned.1.call-update
  19.1 24.5 %all-gather.2.cloned.1.call-done = f32[32,64,128]{2,1,0:T(8,128)} async-done(((f32[4,64,128]{2,1,0:T(8,128)}), f32[32,64,128]{2,1,0:T(8,128)}) %all-gather.2.cloned.1.call-update) | async-done | bytes 1048592 | tf_op jit(solution)/shard_map/while/body/eval_jaxpr/all_gather | solution.py:44
  43.6 1.3 collective-permute-start
  44.9 13.6 %collective-permute-done = f32[4,64,128]{2,1,0:T(8,128)S(1)} collective-permute-done((f32[4,64,128]{2,1,0:T(8,128)S(1)}, f32[4,64,128]{2,1,0:T(8,128)S(1)}, u32[]{:S(2)}, u32[]{:S(2)}) %collective-permute-start) | collective-permute-done | bytes 131104 | tf_op jit(solution)/shard_map/while/body/eval_jaxpr/ppermute | solution.py:12
  58.5 0.0 all-gather.2.cloned.1.call-start
  58.5 1.6 dynamic-slice_select_fusion.2
  60.1 0.0 all-gather.2.cloned.1.call-update
  60.1 23.1 %all-gather.2.cloned.1.call-done = f32[32,64,128]{2,1,0:T(8,128)} async-done(((f32[4,64,128]{2,1,0:T(8,128)}), f32[32,64,128]{2,1,0:T(8,128)}) %all-gather.2.cloned.1.call-update) | async-done | bytes 1048592 | tf_op jit(solution)/shard_map/while/body/eval_jaxpr/all_gather | solution.py:44
  83.2 9.7 %conditional.2 = (f32[4,64,128]{2,1,0:T(8,128)S(1)}) conditional(s32[]{:T(128)} %convert_element_type.9, () %tuple.42, (s32[4,16]{1,0:T(4,128)S(1)}, f32[32,64,128]{2,1,0:T(8,128)}, f32[4,128,16,128]{3,1,2,0:T(8,128)}, s32[]{:T(128)}, f32[4,256,128]{2,1,0:T(8,128)}, /*index=5*/f32[4,128,128]{2,1,0:T(8,128)S(1)}) %tuple.43), branch_computations={%region_1.1_spmd, %region_2.2_spmd} | conditional | flops 855672000 | bytes 11277870 | solution.py:45
  83.2 0.1 reshape.6
  83.3 1.9 gather_fusion
  85.2 6.2 %convolution_bitcast_fusion = f32[4,64,128]{2,1,0:T(8,128)S(1)} fusion(f32[4,16,64,128]{3,2,1,0:T(8,128)S(1)} %bitcast.8, f32[4,128,16,128]{3,1,2,0:T(8,128)} %get-tuple-element.210), kind=kOutput, calls=%fused_computation.2 | convolution fusion | flops 805306368 | bytes 6422528 | tf_op jit(solution)/shard_map/while/body/eval_jaxpr/cond/branch_1_fun/jakb,jkwb->jwa/dot_general | solution.py:28
  91.4 1.5 convolution_add_fusion
  92.9 1.3 collective-permute-start
  94.3 5.4 %collective-permute-done = f32[4,64,128]{2,1,0:T(8,128)S(1)} collective-permute-done((f32[4,64,128]{2,1,0:T(8,128)S(1)}, f32[4,64,128]{2,1,0:T(8,128)S(1)}, u32[]{:S(2)}, u32[]{:S(2)}) %collective-permute-start) | collective-permute-done | bytes 131104 | tf_op jit(solution)/shard_map/while/body/eval_jaxpr/ppermute | solution.py:12
  99.7 0.0 all-gather.2.cloned.1.call-start
  99.7 1.6 dynamic-slice_select_fusion.2
  101.2 0.0 all-gather.2.cloned.1.call-update
  101.3 23.4 %all-gather.2.cloned.1.call-done = f32[32,64,128]{2,1,0:T(8,128)} async-done(((f32[4,64,128]{2,1,0:T(8,128)}), f32[32,64,128]{2,1,0:T(8,128)}) %all-gather.2.cloned.1.call-update) | async-done | bytes 1048592 | tf_op jit(solution)/shard_map/while/body/eval_jaxpr/all_gather | solution.py:44
  124.7 9.7 %conditional.2 = (f32[4,64,128]{2,1,0:T(8,128)S(1)}) conditional(s32[]{:T(128)} %convert_element_type.9, () %tuple.42, (s32[4,16]{1,0:T(4,128)S(1)}, f32[32,64,128]{2,1,0:T(8,128)}, f32[4,128,16,128]{3,1,2,0:T(8,128)}, s32[]{:T(128)}, f32[4,256,128]{2,1,0:T(8,128)}, /*index=5*/f32[4,128,128]{2,1,0:T(8,128)S(1)}) %tuple.43), branch_computations={%region_1.1_spmd, %region_2.2_spmd} | conditional | flops 855672000 | bytes 11277870 | solution.py:45
  124.7 0.1 reshape.6
  124.8 1.9 gather_fusion
  126.7 6.2 %convolution_bitcast_fusion = f32[4,64,128]{2,1,0:T(8,128)S(1)} fusion(f32[4,16,64,128]{3,2,1,0:T(8,128)S(1)} %bitcast.8, f32[4,128,16,128]{3,1,2,0:T(8,128)} %get-tuple-element.210), kind=kOutput, calls=%fused_computation.2 | convolution fusion | flops 805306368 | bytes 6422528 | tf_op jit(solution)/shard_map/while/body/eval_jaxpr/cond/branch_1_fun/jakb,jkwb->jwa/dot_general | solution.py:28
  132.9 1.5 convolution_add_fusion
  134.4 1.3 collective-permute-start
  135.7 5.4 %collective-permute-done = f32[4,64,128]{2,1,0:T(8,128)S(1)} collective-permute-done((f32[4,64,128]{2,1,0:T(8,128)S(1)}, f32[4,64,128]{2,1,0:T(8,128)S(1)}, u32[]{:S(2)}, u32[]{:S(2)}) %collective-permute-start) | collective-permute-done | bytes 131104 | tf_op jit(solution)/shard_map/while/body/eval_jaxpr/ppermute | solution.py:12
  141.1 0.0 all-gather.2.cloned.1.call-start
  141.1 1.6 dynamic-slice_select_fusion.2
  142.7 0.0 all-gather.2.cloned.1.call-update
  142.7 23.1 %all-gather.2.cloned.1.call-done = f32[32,64,128]{2,1,0:T(8,128)} async-done(((f32[4,64,128]{2,1,0:T(8,128)}), f32[32,64,128]{2,1,0:T(8,128)}) %all-gather.2.cloned.1.call-update) | async-done | bytes 1048592 | tf_op jit(solution)/shard_map/while/body/eval_jaxpr/all_gather | solution.py:44
  165.8 9.7 %conditional.2 = (f32[4,64,128]{2,1,0:T(8,128)S(1)}) conditional(s32[]{:T(128)} %convert_element_type.9, () %tuple.42, (s32[4,16]{1,0:T(4,128)S(1)}, f32[32,64,128]{2,1,0:T(8,128)}, f32[4,128,16,128]{3,1,2,0:T(8,128)}, s32[]{:T(128)}, f32[4,256,128]{2,1,0:T(8,128)}, /*index=5*/f32[4,128,128]{2,1,0:T(8,128)S(1)}) %tuple.43), branch_computations={%region_1.1_spmd, %region_2.2_spmd} | conditional | flops 855672000 | bytes 11277870 | solution.py:45
  165.8 0.1 reshape.6
  165.9 1.9 gather_fusion
  167.8 6.2 %convolution_bitcast_fusion = f32[4,64,128]{2,1,0:T(8,128)S(1)} fusion(f32[4,16,64,128]{3,2,1,0:T(8,128)S(1)} %bitcast.8, f32[4,128,16,128]{3,1,2,0:T(8,128)} %get-tuple-element.210), kind=kOutput, calls=%fused_computation.2 | convolution fusion | flops 805306368 | bytes 6422528 | tf_op jit(solution)/shard_map/while/body/eval_jaxpr/cond/branch_1_fun/jakb,jkwb->jwa/dot_general | solution.py:28
  174.0 1.5 convolution_add_fusion
  175.6 1.3 collective-permute-start
  176.9 5.4 %collective-permute-done = f32[4,64,128]{2,1,0:T(8,128)S(1)} collective-permute-done((f32[4,64,128]{2,1,0:T(8,128)S(1)}, f32[4,64,128]{2,1,0:T(8,128)S(1)}, u32[]{:S(2)}, u32[]{:S(2)}) %collective-permute-start) | collective-permute-done | bytes 131104 | tf_op jit(solution)/shard_map/while/body/eval_jaxpr/ppermute | solution.py:12
  182.3 0.0 all-gather.2.cloned.1.call-start
  182.3 1.6 dynamic-slice_select_fusion.2
  183.8 0.0 all-gather.2.cloned.1.call-update
  183.9 23.1 %all-gather.2.cloned.1.call-done = f32[32,64,128]{2,1,0:T(8,128)} async-done(((f32[4,64,128]{2,1,0:T(8,128)}), f32[32,64,128]{2,1,0:T(8,128)}) %all-gather.2.cloned.1.call-update) | async-done | bytes 1048592 | tf_op jit(solution)/shard_map/while/body/eval_jaxpr/all_gather | solution.py:44
  207.0 9.7 %conditional.2 = (f32[4,64,128]{2,1,0:T(8,128)S(1)}) conditional(s32[]{:T(128)} %convert_element_type.9, () %tuple.42, (s32[4,16]{1,0:T(4,128)S(1)}, f32[32,64,128]{2,1,0:T(8,128)}, f32[4,128,16,128]{3,1,2,0:T(8,128)}, s32[]{:T(128)}, f32[4,256,128]{2,1,0:T(8,128)}, /*index=5*/f32[4,128,128]{2,1,0:T(8,128)S(1)}) %tuple.43), branch_computations={%region_1.1_spmd, %region_2.2_spmd} | conditional | flops 855672000 | bytes 11277870 | solution.py:45
  207.0 0.1 reshape.6
  207.1 1.9 gather_fusion
  209.0 6.2 %convolution_bitcast_fusion = f32[4,64,128]{2,1,0:T(8,128)S(1)} fusion(f32[4,16,64,128]{3,2,1,0:T(8,128)S(1)} %bitcast.8, f32[4,128,16,128]{3,1,2,0:T(8,128)} %get-tuple-element.210), kind=kOutput, calls=%fused_computation.2 | convolution fusion | flops 805306368 | bytes 6422528 | tf_op jit(solution)/shard_map/while/body/eval_jaxpr/cond/branch_1_fun/jakb,jkwb->jwa/dot_general | solution.py:28
  215.2 1.5 convolution_add_fusion
  216.7 1.3 collective-permute-start
  218.0 5.4 %collective-permute-done = f32[4,64,128]{2,1,0:T(8,128)S(1)} collective-permute-done((f32[4,64,128]{2,1,0:T(8,128)S(1)}, f32[4,64,128]{2,1,0:T(8,128)S(1)}, u32[]{:S(2)}, u32[]{:S(2)}) %collective-permute-start) | collective-permute-done | bytes 131104 | tf_op jit(solution)/shard_map/while/body/eval_jaxpr/ppermute | solution.py:12
  223.4 0.0 copy-start.1
  223.4 0.8 copy-done.1
  (17 shorter events, 0.3 us)
Async XLA Ops:
  11.9 5.4 %copy-start = (f32[4,128,128]{2,1,0:T(8,128)S(1)}, f32[4,128,128]{2,1,0:T(8,128)}, u32[]{:S(2)}) copy-start(f32[4,128,128]{2,1,0:T(8,128)} %param.11) | copy-start | bytes 786436
  11.9 5.5 %copy-start.2 = (s32[4,16]{1,0:T(4,128)S(1)}, s32[4,16]{1,0:T(4,128)}, u32[]{:S(2)}) copy-start(s32[4,16]{1,0:T(4,128)} %param.9) | copy-start | bytes 772
  17.4 26.2 %all-gather.2.cloned.1.call-start = ((), (), s32[]{:S(2)}) async-start(), calls=%async_computation | async-start | bytes 1179648 | tf_op jit(solution)/shard_map/while/body/eval_jaxpr/all_gather | solution.py:44
  43.6 14.9 %collective-permute-start = (f32[4,64,128]{2,1,0:T(8,128)S(1)}, f32[4,64,128]{2,1,0:T(8,128)S(1)}, u32[]{:S(2)}, u32[]{:S(2)}) collective-permute-start(f32[4,64,128]{2,1,0:T(8,128)S(1)} %get-tuple-element.376), channel_id=1, source_target_pairs={{0,8},{1,9},{2,10},{3,11},{4,12},{5,13},{6,14},{7,15},{16,24},{17,... | collective-permute-start | bytes 393224 | tf_op jit(solution)/shard_map/while/body/eval_jaxpr/ppermute | solution.py:12
  58.5 24.7 %all-gather.2.cloned.1.call-start = ((), (), s32[]{:S(2)}) async-start(), calls=%async_computation | async-start | bytes 1179648 | tf_op jit(solution)/shard_map/while/body/eval_jaxpr/all_gather | solution.py:44
  92.9 6.7 %collective-permute-start = (f32[4,64,128]{2,1,0:T(8,128)S(1)}, f32[4,64,128]{2,1,0:T(8,128)S(1)}, u32[]{:S(2)}, u32[]{:S(2)}) collective-permute-start(f32[4,64,128]{2,1,0:T(8,128)S(1)} %get-tuple-element.376), channel_id=1, source_target_pairs={{0,8},{1,9},{2,10},{3,11},{4,12},{5,13},{6,14},{7,15},{16,24},{17,... | collective-permute-start | bytes 393224 | tf_op jit(solution)/shard_map/while/body/eval_jaxpr/ppermute | solution.py:12
  99.7 25.0 %all-gather.2.cloned.1.call-start = ((), (), s32[]{:S(2)}) async-start(), calls=%async_computation | async-start | bytes 1179648 | tf_op jit(solution)/shard_map/while/body/eval_jaxpr/all_gather | solution.py:44
  134.4 6.7 %collective-permute-start = (f32[4,64,128]{2,1,0:T(8,128)S(1)}, f32[4,64,128]{2,1,0:T(8,128)S(1)}, u32[]{:S(2)}, u32[]{:S(2)}) collective-permute-start(f32[4,64,128]{2,1,0:T(8,128)S(1)} %get-tuple-element.376), channel_id=1, source_target_pairs={{0,8},{1,9},{2,10},{3,11},{4,12},{5,13},{6,14},{7,15},{16,24},{17,... | collective-permute-start | bytes 393224 | tf_op jit(solution)/shard_map/while/body/eval_jaxpr/ppermute | solution.py:12
  141.1 24.7 %all-gather.2.cloned.1.call-start = ((), (), s32[]{:S(2)}) async-start(), calls=%async_computation | async-start | bytes 1179648 | tf_op jit(solution)/shard_map/while/body/eval_jaxpr/all_gather | solution.py:44
  175.6 6.7 %collective-permute-start = (f32[4,64,128]{2,1,0:T(8,128)S(1)}, f32[4,64,128]{2,1,0:T(8,128)S(1)}, u32[]{:S(2)}, u32[]{:S(2)}) collective-permute-start(f32[4,64,128]{2,1,0:T(8,128)S(1)} %get-tuple-element.376), channel_id=1, source_target_pairs={{0,8},{1,9},{2,10},{3,11},{4,12},{5,13},{6,14},{7,15},{16,24},{17,... | collective-permute-start | bytes 393224 | tf_op jit(solution)/shard_map/while/body/eval_jaxpr/ppermute | solution.py:12
  182.3 24.7 %all-gather.2.cloned.1.call-start = ((), (), s32[]{:S(2)}) async-start(), calls=%async_computation | async-start | bytes 1179648 | tf_op jit(solution)/shard_map/while/body/eval_jaxpr/all_gather | solution.py:44
  216.7 6.7 %collective-permute-start = (f32[4,64,128]{2,1,0:T(8,128)S(1)}, f32[4,64,128]{2,1,0:T(8,128)S(1)}, u32[]{:S(2)}, u32[]{:S(2)}) collective-permute-start(f32[4,64,128]{2,1,0:T(8,128)S(1)} %get-tuple-element.376), channel_id=1, source_target_pairs={{0,8},{1,9},{2,10},{3,11},{4,12},{5,13},{6,14},{7,15},{16,24},{17,... | collective-permute-start | bytes 393224 | tf_op jit(solution)/shard_map/while/body/eval_jaxpr/ppermute | solution.py:12
  223.4 0.8 copy-start.1
Sparse Core Ops, SparseCore 0:
  19.8 23.7 all-gather.1
  60.9 22.2 all-gather.1
  102.1 22.5 all-gather.1
  143.2 22.5 all-gather.1
  184.4 22.5 all-gather.1
where the time goes:
time: 232 us; the launch traced here: 231 us
  waiting for transfers between devices  152 us (66%)
  matrix products  30.8 us (13%)
  local copies, waits for them, and re-layouts  19.6 us (8%)
  between operations  13.1 us (6%)
  other arithmetic  8.07 us (3%)
  starting transfers between devices  6.51 us (3%)
    all_gather x5, waiting for transfers between devices, section(): previous = lax.all_gather(source, 'lat', axis=0, tiled=True)  117 us
    ppermute x5, waiting for transfers between devices, passed_along(): return lax.ppermute(array, axis, pairs)  35.1 us
    dot_general x4, matrix products, compute(): jnp.einsum('jakb,jkwb->jwa', factors, picked, precision=lax.Precision.HIG...  24.7 us
    select_n x5, other arithmetic, section(): source = jnp.where(slab_pos == 0, boundary, incoming)  7.89 us
    gather x4, local copies, waits for them, and re-layouts, compute(): picked = previous[cond_lists]  7.62 us
    ppermute x5, starting transfers between devices, passed_along(): return lax.ppermute(array, axis, pairs)  6.46 us
    unnamed x7, local copies, waits for them, and re-layouts  6.15 us
    dot_general x4, matrix products, compute(): jnp.einsum('jab,jwb->jwa', chol, shocks, precision=lax.Precision.HIGHEST)  6.13 us
  transfers between devices with their start and end apart: 10, of which 10 were waited for; matrix products, arithmetic and copies ran while one was open for 0% of the time, Pallas kernels for 0%

commit v1 on v0

v1 whole, which is shorter than its diff:
```python
import functools

import jax
import jax.numpy as jnp
from jax import lax
from jax.experimental import pallas as pl
from jax.experimental.pallas import tpu as pltpu
from jax.sharding import PartitionSpec as P

MESH = pl.DeviceIdType.MESH
FRONT = 32
LEAD = 2


def halves(x):
    high = x.astype(jnp.bfloat16)
    low = (x - high.astype(jnp.float32)).astype(jnp.bfloat16)
    return high, low


def folded(product, rows, columns):
    small = product[:rows, columns:] + product[rows:, :columns] + product[rows:, columns:]
    return product[:rows, :columns] + small


def kernel(
    n_slab, n_lat, front,
    cond, regress_hbm, chol_ref, noise_ref, start_hbm, out_ref,
    held, factors, weights, split,
    start_sem, factor_sem,
    lane_send, lane_recv, end_send, pair_send, pair_recv, slab_send, slab_recv,
):
    blocks, nreal, size = noise_ref.shape
    listed = regress_hbm.shape[2] // size
    fronts = nreal // front
    chips = n_lat // 2
    slab = lax.axis_index("slab")
    lat = lax.axis_index("lat")
    chip, core = lax.div(lat, 2), lax.rem(lat, 2)
    first, last = slab == 0, slab == n_slab - 1

    def lat_of(other_chip, other_core):
        return other_chip * 2 + other_core

    def chunk(f, of_lat):
        return held.at[f, pl.ds(of_lat * blocks, blocks)]

    def start_copy(f):
        return pltpu.make_async_copy(
            start_hbm.at[:, pl.ds(f * front, front)], chunk(f, lat), start_sem.at[f]
        )

    def factor_copy(j):
        return pltpu.make_async_copy(regress_hbm.at[j], factors.at[j], factor_sem.at[j])

    @pl.when(first)
    def _():
        for f in range(fronts):
            start_copy(f).start()

    for j in range(blocks):
        factor_copy(j).start()

    barrier = pltpu.get_barrier_semaphore()

    def greet(**where):
        pl.semaphore_signal(barrier, inc=1, device_id=where, device_id_type=MESH)

    for o in range(1, chips):
        greet(lat=lat_of(lax.rem(chip + o, chips), core))
    greet(lat=lat_of(chip, 1 - core))

    @pl.when(jnp.logical_not(first))
    def _():
        greet(slab=slab - 1)

    @pl.when(jnp.logical_not(last))
    def _():
        greet(slab=slab + 1)

    partners = chips + jnp.where(first, 0, 1) + jnp.where(last, 0, 1)
    pl.semaphore_wait(barrier, partners)

    def lane_copy(f, o):
        return pltpu.make_async_remote_copy(
            src_ref=chunk(f, lat), dst_ref=chunk(f, lat),
            send_sem=lane_send.at[f, o], recv_sem=lane_recv.at[f, o],
            device_id={"lat": lat_of(lax.rem(chip + o, chips), core)}, device_id_type=MESH,
        )

    def lane_arrival(f, o):
        source = lat_of(lax.rem(chip + chips - o, chips), core)
        return pltpu.make_async_remote_copy(
            src_ref=chunk(f, source), dst_ref=chunk(f, source),
            send_sem=lane_send.at[f, o], recv_sem=lane_recv.at[f, o],
            device_id={"lat": lat_of(lax.rem(chip + o, chips), core)}, device_id_type=MESH,
        )

    def end_copy(f, source_chip, target_chip):
        o = (target_chip - source_chip) % chips
        source = lat_of(source_chip, core)
        return pltpu.make_async_remote_copy(
            src_ref=chunk(f, source), dst_ref=chunk(f, source),
            send_sem=end_send.at[f, 0 if source_chip == 0 else 1], recv_sem=lane_recv.at[f, o],
            device_id={"lat": lat_of(target_chip, core)}, device_id_type=MESH,
        )

    def pair_copy(f, o):
        source = lat_of(lax.rem(chip + chips - o, chips), core)
        return pltpu.make_async_remote_copy(
            src_ref=chunk(f, source), dst_ref=chunk(f, source),
            send_sem=pair_send.at[f, o], recv_sem=pair_recv.at[f, o],
            device_id={"lat": lat_of(chip, 1 - core)}, device_id_type=MESH,
        )

    def pair_arrival(f, o):
        source = lat_of(lax.rem(chip + chips - o, chips), 1 - core)
        return pltpu.make_async_remote_copy(
            src_ref=chunk(f, source), dst_ref=chunk(f, source),
            send_sem=pair_send.at[f, o], recv_sem=pair_recv.at[f, o],
            device_id={"lat": lat_of(chip, 1 - core)}, device_id_type=MESH,
        )

    def slab_copy(f):
        return pltpu.make_async_remote_copy(
            src_ref=out_ref.at[:, pl.ds(f * front, front)], dst_ref=chunk(f, lat),
            send_sem=slab_send.at[f], recv_sem=slab_recv.at[f],
            device_id={"slab": lax.rem(slab + 1, n_slab)}, device_id_type=MESH,
        )

    relayed = chips > 2

    def direct(o):
        if not relayed:
            return True
        if o == chips - 1 and o == 1:
            return True
        if o == chips - 1:
            return chip != 0
        if o == 1:
            return chip != chips - 1
        return True

    def guarded(condition, action):
        if condition is True:
            action()
        else:
            pl.when(condition)(action)

    order = sorted(range(1, chips), key=lambda o: -min(o, chips - o))

    def distribute(f):
        @pl.when(first)
        def _():
            start_copy(f).wait()

        @pl.when(jnp.logical_not(first))
        def _():
            slab_copy(f).wait_recv()

        for o in order:
            guarded(direct(o), lambda o=o: lane_copy(f, o).start())
        pair_copy(f, 0).start()

    def hand_on(f):
        for o in order:
            lane_arrival(f, o).wait_recv()
            if relayed and o == chips - 2:
                @pl.when(chip == chips - 2)
                def _():
                    end_copy(f, 0, chips - 1).start()
            if relayed and o == 2:
                @pl.when(chip == 1)
                def _():
                    end_copy(f, chips - 1, 0).start()
            pair_copy(f, o).start()

    def compute(f):
        for o in range(chips):
            pair_arrival(f, o).wait_recv()
        positions = held.shape[1]
        for p in range(positions):
            high, low = halves(held[f, p])
            split[p, :front] = high
            split[p, front:] = low
        rows = pl.ds(pl.multiple_of(f * front, front), front)
        for j in range(blocks):
            picked = jnp.concatenate([split[cond[j, k]] for k in range(listed)], axis=1)
            product = jnp.dot(picked, weights[j], preferred_element_type=jnp.float32)
            out_ref[j, rows] += folded(product, front, size)

        @pl.when(jnp.logical_not(last))
        def _():
            slab_copy(f).start()

    @pl.when(first)
    def _():
        for f in range(min(LEAD, fronts)):
            distribute(f)

    for j in range(blocks):
        high, low = halves(noise_ref[j])
        left = jnp.concatenate([high, low], axis=0)
        high, low = halves(chol_ref[j].T)
        right = jnp.concatenate([high, low], axis=1)
        product = jnp.dot(left, right, preferred_element_type=jnp.float32)
        out_ref[j] = folded(product, nreal, size)

    for j in range(blocks):
        factor_copy(j).wait()

        @pl.loop(0, listed)
        def _(k):
            at = pl.multiple_of(k * size, size)
            high, low = halves(factors[j, :, pl.ds(at, size)].T)
            weights[j, pl.ds(at, size), :size] = high
            weights[j, pl.ds(at, size), size:] = low

    @pl.loop(0, fronts + 1)
    def _(i):
        @pl.when(jnp.logical_and(jnp.logical_not(first), i < fronts))
        def _():
            distribute(i)

        @pl.when(i < fronts)
        def _():
            hand_on(i)

        @pl.when(jnp.logical_and(first, i + LEAD < fronts))
        def _():
            distribute(i + LEAD)

        f = jnp.where(first, i, i - 1)

        @pl.when(jnp.logical_and(f >= 0, f < fronts))
        def _():
            compute(f)

    @pl.loop(0, fronts)
    def _(f):
        for o in range(1, chips):
            guarded(direct(o), lambda o=o: lane_copy(f, o).wait_send())
        for o in range(chips):
            pair_copy(f, o).wait_send()
        if relayed:
            @pl.when(chip == chips - 2)
            def _():
                end_copy(f, 0, chips - 1).wait_send()

            @pl.when(chip == 1)
            def _():
                end_copy(f, chips - 1, 0).wait_send()

        @pl.when(jnp.logical_not(last))
        def _():
            slab_copy(f).wait_send()


def solution(mesh):
    n_slab, n_lat = mesh.shape["slab"], mesh.shape["lat"]
    in_specs = (
        P(("slab", "lat"), None),
        P(("slab", "lat"), None, None),
        P(("slab", "lat"), None, None),
        P(("grp", "slab", "lat"), None, None),
        P(("grp", "lat"), None, None),
    )
    out_specs = P(("grp", "slab", "lat"), None, None)

    def shards(cond_lists, regress, chol, noise, start_field):
        blocks, nreal, size = noise.shape
        width = regress.shape[2]
        positions = blocks * n_lat
        front = min(FRONT, nreal)
        fronts = nreal // front
        chips = n_lat // 2
        vmem = pl.BlockSpec(memory_space=pltpu.VMEM)
        hbm = pl.BlockSpec(memory_space=pl.ANY)
        dma = pltpu.SemaphoreType.DMA
        return pl.pallas_call(
            functools.partial(kernel, n_slab, n_lat, front),
            out_shape=jax.ShapeDtypeStruct(noise.shape, jnp.float32),
            in_specs=[pl.BlockSpec(memory_space=pltpu.SMEM), hbm, vmem, vmem, hbm],
            out_specs=vmem,
            scratch_shapes=[
                pltpu.VMEM((fronts, positions, front, size), jnp.float32),
                pltpu.VMEM((blocks, size, width), jnp.float32),
                pltpu.VMEM((blocks, width, 2 * size), jnp.bfloat16),
                pltpu.VMEM((positions, 2 * front, size), jnp.bfloat16),
                dma((fronts,)),
                dma((blocks,)),
                dma((fronts, chips)),
                dma((fronts, chips)),
                dma((fronts, 2)),
                dma((fronts, chips)),
                dma((fronts, chips)),
                dma((fronts,)),
                dma((fronts,)),
            ],
            compiler_params=pltpu.CompilerParams(
                collective_id=0, has_side_effects=True, vmem_limit_bytes=48 * 1024 * 1024
            ),
            name="evolve",
        )(cond_lists, regress, chol, noise, start_field)

    return jax.shard_map(shards, mesh=mesh, in_specs=in_specs, out_specs=out_specs, check_vma=False)
```

time: 232 us -> 97.2 us (0.42)
  waiting for transfers between devices: 152 us -> 0 us
  Pallas kernels: 0 us -> 90.2 us
  matrix products: 30.8 us -> 0 us
  between operations: 13.1 us -> 0.01 us
  local copies, waits for them, and re-layouts: 19.6 us -> 6.7 us
  other arithmetic: 8.07 us -> 0 us
  starting transfers between devices: 6.51 us -> 0 us
    all_gather x5 -> x0, waiting for transfers between devices: 117 us -> none  [section(): previous = lax.all_gather(source, 'lat', axis=0, tiled=True)]
    pallas_call x0 -> x1, Pallas kernels: none -> 90.2 us  [shards(): pl.pallas_call(functools.partial(kernel, n_slab, n_lat, front), out_shape...]
    ppermute x5 -> x0, waiting for transfers between devices: 35.1 us -> none  [passed_along(): return lax.ppermute(array, axis, pairs)]
    dot_general x8 -> x0, matrix products: 30.8 us -> none  [the longest x4 24.7 us: compute(): jnp.einsum('jakb,jkwb->jwa', factors, picked, precision=lax.Precision.HIG...]
    select_n x9 -> x0, other arithmetic: 7.9 us -> none  [the longest x5 7.89 us: section(): source = jnp.where(slab_pos == 0, boundary, incoming)]
    gather x4 -> x0, local copies, waits for them, and re-layouts: 7.62 us -> none  [compute(): picked = previous[cond_lists]]
    ppermute x5 -> x0, starting transfers between devices: 6.46 us -> none  [passed_along(): return lax.ppermute(array, axis, pairs)]
    while x1 -> x0, local copies, waits for them, and re-layouts: 5.38 us -> none  [shards(): lax.fori_loop(0, sections, section, (start_box, start_out))]
  transfers between devices with their start and end apart: 10 -> 0, of which waited for: 10 -> 0; matrix products, arithmetic and copies ran while one was open for 0% -> 0% of each run, Pallas kernels for 0% -> 0%
where the time goes in v1:
time: 97.2 us; the launch traced here: 96.9 us
  Pallas kernels  90.2 us (93%)
  local copies, waits for them, and re-layouts  6.7 us (7%)
    pallas_call x1, Pallas kernels, shards(): pl.pallas_call(functools.partial(kernel, n_slab, n_lat, front), out_shape...  90.2 us
    unnamed x11, local copies, waits for them, and re-layouts  6.7 us

profile of v1, /device:TPU:3, one launch (start us, length us, event | category | flops | bytes accessed | tf_op | source)
XLA Modules:
  0.0 96.9 jit_solution(16323230114350773583)
XLA Ops:
  0.0 0.0 copy-start
  0.0 2.2 %copy-done = f32[4,128,2048]{2,1,0:T(8,128)S(1)} copy-done((f32[4,128,2048]{2,1,0:T(8,128)S(1)}, f32[4,128,2048]{2,1,0:T(8,128)}, u32[]{:S(2)}) %copy-start) | copy-done | bytes 4194328
  2.2 0.0 copy-start.1
  2.2 1.0 %copy-done.1 = f32[4,256,128]{2,1,0:T(8,128)S(1)} copy-done((f32[4,256,128]{2,1,0:T(8,128)S(1)}, f32[4,256,128]{2,1,0:T(8,128)}, u32[]{:S(2)}) %copy-start.1) | copy-done | bytes 524312
  3.2 0.0 copy-start.2
  3.2 1.0 %copy-done.2 = f32[4,256,128]{2,1,0:T(8,128)S(1)} copy-done((f32[4,256,128]{2,1,0:T(8,128)S(1)}, f32[4,256,128]{2,1,0:T(8,128)}, u32[]{:S(2)}) %copy-start.2) | copy-done | bytes 524312
  4.3 0.0 copy-start.3
  4.3 0.9 copy-done.3
  5.2 0.0 copy-start.4
  5.2 0.7 copy-done.4
  5.9 90.2 %evolve.1 = f32[4,256,128]{2,1,0:T(8,128)S(1)} custom-call(s32[4,16]{1,0:T(4,128)S(1)} %copy-done.4, f32[4,128,2048]{2,1,0:T(8,128)S(1)} %copy-done, f32[4,128,128]{2,1,0:T(8,128)S(1)} %copy-done.3, f32[4,256,128]{2,1,0:T(8,128)S(1)} %copy-done.1, f32[4,256,128]{2,1,0:T(8,128)S(1)} %copy-done.2), custom_call_target="tpu_custom_call" | custom-call | tf_op jit(solution)/shard_map/evolve/pallas_call | solution.py:280
  96.1 0.8 copy.7
Async XLA Ops:
  0.0 2.2 %copy-start = (f32[4,128,2048]{2,1,0:T(8,128)S(1)}, f32[4,128,2048]{2,1,0:T(8,128)}, u32[]{:S(2)}) copy-start(f32[4,128,2048]{2,1,0:T(8,128)} %regress_hbm.1) | copy-start | bytes 12582916
  2.2 1.0 %copy-start.1 = (f32[4,256,128]{2,1,0:T(8,128)S(1)}, f32[4,256,128]{2,1,0:T(8,128)}, u32[]{:S(2)}) copy-start(f32[4,256,128]{2,1,0:T(8,128)} %noise_ref.1) | copy-start | bytes 1572868
  3.2 1.0 %copy-start.2 = (f32[4,256,128]{2,1,0:T(8,128)S(1)}, f32[4,256,128]{2,1,0:T(8,128)}, u32[]{:S(2)}) copy-start(f32[4,256,128]{2,1,0:T(8,128)} %start_hbm.1) | copy-start | bytes 1572868
  4.3 0.9 copy-start.3
  5.2 0.7 copy-start.4

commit v2 on v1

--- a/solution.py
+++ b/solution.py
@@ -8,8 +8,8 @@
 from jax.sharding import PartitionSpec as P
 
 MESH = pl.DeviceIdType.MESH
-FRONT = 32
-LEAD = 2
+FRONT = 64
+LEAD = 1
 
 
 def halves(x):

time: 97.2 us -> 74.2 us (0.76)
  Pallas kernels: 90.2 us -> 67.2 us
    pallas_call x1, Pallas kernels: 90.2 us -> 67.2 us  [shards(): pl.pallas_call(functools.partial(kernel, n_slab, n_lat, front), out_shape...]
where the time goes in v2:
time: 74.2 us; the launch traced here: 73.9 us
  Pallas kernels  67.2 us (91%)
  local copies, waits for them, and re-layouts  6.7 us (9%)
    pallas_call x1, Pallas kernels, shards(): pl.pallas_call(functools.partial(kernel, n_slab, n_lat, front), out_shape...  67.2 us
    unnamed x11, local copies, waits for them, and re-layouts  6.7 us

profile of v2, /device:TPU:3, one launch (start us, length us, event | category | flops | bytes accessed | tf_op | source)
XLA Modules:
  0.0 73.9 jit_solution(8297867608768596244)
XLA Ops:
  0.0 0.0 copy-start
  0.0 2.2 %copy-done = f32[4,128,2048]{2,1,0:T(8,128)S(1)} copy-done((f32[4,128,2048]{2,1,0:T(8,128)S(1)}, f32[4,128,2048]{2,1,0:T(8,128)}, u32[]{:S(2)}) %copy-start) | copy-done | bytes 4194328
  2.2 0.0 copy-start.1
  2.2 1.0 %copy-done.1 = f32[4,256,128]{2,1,0:T(8,128)S(1)} copy-done((f32[4,256,128]{2,1,0:T(8,128)S(1)}, f32[4,256,128]{2,1,0:T(8,128)}, u32[]{:S(2)}) %copy-start.1) | copy-done | bytes 524312
  3.2 0.0 copy-start.2
  3.2 1.0 %copy-done.2 = f32[4,256,128]{2,1,0:T(8,128)S(1)} copy-done((f32[4,256,128]{2,1,0:T(8,128)S(1)}, f32[4,256,128]{2,1,0:T(8,128)}, u32[]{:S(2)}) %copy-start.2) | copy-done | bytes 524312
  4.3 0.0 copy-start.3
  4.3 0.9 %copy-done.3 = f32[4,128,128]{2,1,0:T(8,128)S(1)} copy-done((f32[4,128,128]{2,1,0:T(8,128)S(1)}, f32[4,128,128]{2,1,0:T(8,128)}, u32[]{:S(2)}) %copy-start.3) | copy-done | bytes 262168
  5.2 0.0 copy-start.4
  5.2 0.7 copy-done.4
  5.9 67.2 %evolve.1 = f32[4,256,128]{2,1,0:T(8,128)S(1)} custom-call(s32[4,16]{1,0:T(4,128)S(1)} %copy-done.4, f32[4,128,2048]{2,1,0:T(8,128)S(1)} %copy-done, f32[4,128,128]{2,1,0:T(8,128)S(1)} %copy-done.3, f32[4,256,128]{2,1,0:T(8,128)S(1)} %copy-done.1, f32[4,256,128]{2,1,0:T(8,128)S(1)} %copy-done.2), custom_call_target="tpu_custom_call" | custom-call | tf_op jit(solution)/shard_map/evolve/pallas_call | solution.py:280
  73.1 0.8 %copy.7 = f32[4,256,128]{2,1,0:T(8,128)} copy(f32[4,256,128]{2,1,0:T(8,128)S(1)} %evolve.1) | data formatting | bytes 1048576
Async XLA Ops:
  0.0 2.2 %copy-start = (f32[4,128,2048]{2,1,0:T(8,128)S(1)}, f32[4,128,2048]{2,1,0:T(8,128)}, u32[]{:S(2)}) copy-start(f32[4,128,2048]{2,1,0:T(8,128)} %regress_hbm.1) | copy-start | bytes 12582916
  2.2 1.0 %copy-start.1 = (f32[4,256,128]{2,1,0:T(8,128)S(1)}, f32[4,256,128]{2,1,0:T(8,128)}, u32[]{:S(2)}) copy-start(f32[4,256,128]{2,1,0:T(8,128)} %noise_ref.1) | copy-start | bytes 1572868
  3.2 1.0 %copy-start.2 = (f32[4,256,128]{2,1,0:T(8,128)S(1)}, f32[4,256,128]{2,1,0:T(8,128)}, u32[]{:S(2)}) copy-start(f32[4,256,128]{2,1,0:T(8,128)} %start_hbm.1) | copy-start | bytes 1572868
  4.3 0.9 %copy-start.3 = (f32[4,128,128]{2,1,0:T(8,128)S(1)}, f32[4,128,128]{2,1,0:T(8,128)}, u32[]{:S(2)}) copy-start(f32[4,128,128]{2,1,0:T(8,128)} %chol_ref.1) | copy-start | bytes 786436
  5.2 0.7 copy-start.4

commit v3 on v2

--- a/solution.py
+++ b/solution.py
@@ -162,18 +162,26 @@
             guarded(direct(o), lambda o=o: lane_copy(f, o).start())
         pair_copy(f, 0).start()
 
+    relays = [o for o in order if relayed and o in (2, chips - 2)]
+
     def hand_on(f):
-        for o in order:
+        for o in relays:
             lane_arrival(f, o).wait_recv()
-            if relayed and o == chips - 2:
+            if o == chips - 2:
                 @pl.when(chip == chips - 2)
                 def _():
                     end_copy(f, 0, chips - 1).start()
-            if relayed and o == 2:
+            if o == 2:
                 @pl.when(chip == 1)
                 def _():
                     end_copy(f, chips - 1, 0).start()
             pair_copy(f, o).start()
+
+    def share(f):
+        for o in order:
+            if o not in relays:
+                lane_arrival(f, o).wait_recv()
+                pair_copy(f, o).start()
 
     def compute(f):
         for o in range(chips):
@@ -234,6 +242,7 @@
 
         @pl.when(jnp.logical_and(f >= 0, f < fronts))
         def _():
+            share(f)
             compute(f)
 
     @pl.loop(0, fronts)

time: 74.2 us -> 69.9 us (0.942)
  Pallas kernels: 67.2 us -> 62.8 us
    pallas_call x1, Pallas kernels: 67.2 us -> 62.8 us  [shards(): pl.pallas_call(functools.partial(kernel, n_slab, n_lat, front), out_shape...]
where the time goes in v3:
time: 69.9 us; the launch traced here: 69.6 us
  Pallas kernels  62.8 us (90%)
  local copies, waits for them, and re-layouts  6.7 us (10%)
    pallas_call x1, Pallas kernels, shards(): pl.pallas_call(functools.partial(kernel, n_slab, n_lat, front), out_shape...  62.8 us
    unnamed x11, local copies, waits for them, and re-layouts  6.7 us

profile of v3, /device:TPU:3, one launch (start us, length us, event | category | flops | bytes accessed | tf_op | source)
XLA Modules:
  0.0 69.6 jit_solution(3695908885921813074)
XLA Ops:
  0.0 0.0 copy-start
  0.0 2.2 %copy-done = f32[4,128,2048]{2,1,0:T(8,128)S(1)} copy-done((f32[4,128,2048]{2,1,0:T(8,128)S(1)}, f32[4,128,2048]{2,1,0:T(8,128)}, u32[]{:S(2)}) %copy-start) | copy-done | bytes 4194328
  2.2 0.0 copy-start.1
  2.2 1.0 %copy-done.1 = f32[4,256,128]{2,1,0:T(8,128)S(1)} copy-done((f32[4,256,128]{2,1,0:T(8,128)S(1)}, f32[4,256,128]{2,1,0:T(8,128)}, u32[]{:S(2)}) %copy-start.1) | copy-done | bytes 524312
  3.2 0.0 copy-start.2
  3.2 1.0 %copy-done.2 = f32[4,256,128]{2,1,0:T(8,128)S(1)} copy-done((f32[4,256,128]{2,1,0:T(8,128)S(1)}, f32[4,256,128]{2,1,0:T(8,128)}, u32[]{:S(2)}) %copy-start.2) | copy-done | bytes 524312
  4.3 0.0 copy-start.3
  4.3 0.9 %copy-done.3 = f32[4,128,128]{2,1,0:T(8,128)S(1)} copy-done((f32[4,128,128]{2,1,0:T(8,128)S(1)}, f32[4,128,128]{2,1,0:T(8,128)}, u32[]{:S(2)}) %copy-start.3) | copy-done | bytes 262168
  5.2 0.0 copy-start.4
  5.2 0.7 copy-done.4
  5.9 62.8 %evolve.1 = f32[4,256,128]{2,1,0:T(8,128)S(1)} custom-call(s32[4,16]{1,0:T(4,128)S(1)} %copy-done.4, f32[4,128,2048]{2,1,0:T(8,128)S(1)} %copy-done, f32[4,128,128]{2,1,0:T(8,128)S(1)} %copy-done.3, f32[4,256,128]{2,1,0:T(8,128)S(1)} %copy-done.1, f32[4,256,128]{2,1,0:T(8,128)S(1)} %copy-done.2), custom_call_target="tpu_custom_call" | custom-call | tf_op jit(solution)/shard_map/evolve/pallas_call | solution.py:289
  68.8 0.8 %copy.7 = f32[4,256,128]{2,1,0:T(8,128)} copy(f32[4,256,128]{2,1,0:T(8,128)S(1)} %evolve.1) | data formatting | bytes 1048576
Async XLA Ops:
  0.0 2.2 %copy-start = (f32[4,128,2048]{2,1,0:T(8,128)S(1)}, f32[4,128,2048]{2,1,0:T(8,128)}, u32[]{:S(2)}) copy-start(f32[4,128,2048]{2,1,0:T(8,128)} %regress_hbm.1) | copy-start | bytes 12582916
  2.2 1.0 %copy-start.1 = (f32[4,256,128]{2,1,0:T(8,128)S(1)}, f32[4,256,128]{2,1,0:T(8,128)}, u32[]{:S(2)}) copy-start(f32[4,256,128]{2,1,0:T(8,128)} %noise_ref.1) | copy-start | bytes 1572868
  3.2 1.0 %copy-start.2 = (f32[4,256,128]{2,1,0:T(8,128)S(1)}, f32[4,256,128]{2,1,0:T(8,128)}, u32[]{:S(2)}) copy-start(f32[4,256,128]{2,1,0:T(8,128)} %start_hbm.1) | copy-start | bytes 1572868
  4.3 0.9 %copy-start.3 = (f32[4,128,128]{2,1,0:T(8,128)S(1)}, f32[4,128,128]{2,1,0:T(8,128)}, u32[]{:S(2)}) copy-start(f32[4,128,128]{2,1,0:T(8,128)} %chol_ref.1) | copy-start | bytes 786436
  5.2 0.7 copy-start.4
